TPU v7x, 512 devices: a whole 4x8x8 slice. The times are simulated.
512 devices in a mesh: row: 64 (over x, y, core), col: 8 (over z).
Axes of the slice: x: 4, y: 8, z: 8, core: 2. Of those that a mesh axis runs over, the one named last changes fastest.
Arguments:
- panel: bfloat16 [262144, 256], P('row'), may hold values from -400 to 400, as said below
- slab: bfloat16 [262144, 1024], P('row', 'col'), may hold values from -300 to 300
Outputs:
- factor: float32 [256, 256], P(None, 'col')
- coupling: float32 [256, 1024], P(None, 'col')
- remainder: bfloat16 [262144, 1024], P('row', 'col')
Inputs may be any that keep to these rules, and one draw needn't show every extreme that they name: panel has full column rank.
All inputs are finite; a program needn't handle non-finite values.
Results may differ from a plain program's by a relative error of at most 0.015.
The roundings to bfloat16 on the way count: a program that leaves them out, or rounds other values in their place, can miss the bound.
Values sent between devices are 32-bit elements; how exact they have to be, the bound alone decides.
No kernel may reach another device: no remote copies, remote signals or barrier semaphores. Data moves between devices by JAX's collectives and lax.ppermute only.
A program may use at most 64 MiB of HBM per device.

v0:
```python
import jax
import jax.numpy as jnp
from jax import lax
from jax.sharding import PartitionSpec as P


def in_one(arrays, axis):
    vector, at, gathered = (jnp.concatenate([a.reshape(-1) for a in arrays]), 0, [])
    running = lax.psum(vector, axis)
    for a in arrays:
        gathered.append(running[at : at + a.size].reshape(a.shape))
        at += a.size
    return tuple(gathered)


def matmul(left, right):
    return jnp.dot(left, right, precision=lax.Precision.HIGHEST)


def factor_inverse(gram):
    order = gram.shape[0]
    if order == 1:
        root = jnp.sqrt(gram)
        return (root, 1.0 / root)
    half = order // 2
    upper_left, upper_inv = factor_inverse(gram[:half, :half])
    coupled = matmul(upper_inv.T, gram[:half, half:])
    lower_right, lower_inv = factor_inverse(gram[half:, half:] - matmul(coupled.T, coupled))
    zeros_block = jnp.zeros((order - half, half), gram.dtype)
    whole = jnp.concatenate(
        [
            jnp.concatenate([upper_left, coupled], axis=1),
            jnp.concatenate([zeros_block, lower_right], axis=1),
        ],
        axis=0,
    )
    corner = -matmul(matmul(upper_inv, coupled), lower_inv)
    inverse = jnp.concatenate(
        [
            jnp.concatenate([upper_inv, corner], axis=1),
            jnp.concatenate([zeros_block, lower_inv], axis=1),
        ],
        axis=0,
    )
    return (whole, inverse)


def upper_factor(gram):
    return factor_inverse(gram)[0]


def on_device(panel, slab):
    total_rows = panel.shape[0] * lax.axis_size("row")
    scale = 1.0 / total_rows
    contract = (((0,), (0,)), ((), ()))
    local_gram = lax.dot_general(panel, panel, contract, preferred_element_type=jnp.float32) * scale
    local_cross = lax.dot_general(panel, slab, contract, preferred_element_type=jnp.float32) * scale
    gram, cross = in_one((local_gram, local_cross), "row")
    factor = upper_factor(gram)
    inverse = factor_inverse(matmul(factor.T, factor))[1]
    coupling = matmul(inverse.T, cross)
    update = matmul(inverse, coupling).astype(jnp.bfloat16)
    remainder = (
        slab.astype(jnp.float32) - jnp.dot(panel, update, preferred_element_type=jnp.float32)
    ).astype(jnp.bfloat16)
    share = factor.shape[1] // lax.axis_size("col")
    factor_part = lax.dynamic_slice_in_dim(factor, lax.axis_index("col") * share, share, 1)
    return (factor_part, coupling, remainder)


def solution(mesh):
    return jax.shard_map(
        on_device,
        mesh=mesh,
        in_specs=(P("row", None), P("row", "col")),
        out_specs=(P(None, "col"), P(None, "col"), P("row", "col")),
        check_vma=False,
    )
```

profile of v0, /device:TPU:1, one launch (start us, length us, event | category | flops | bytes accessed | tf_op | source)
XLA Modules:
  0.0 1166.5 jit_solution(4382981189412300618)
XLA Ops:
  7.2 1.5 copy-done
  11.2 1.3 copy.270
  12.5 194.3 %all-reduce.376.cloned.1.call-done = f32[98304]{0:T(1024)} async-done(((f32[98304]{0:T(1024)}), f32[98304]{0:T(1024)}) %all-reduce.376.cloned.1.call-update) | async-done | bytes 393232 | tf_op jit(solution)/shard_map/psum | solution.py:9
  206.8 1.0 slice.6150
  909.0 0.8 fusion.3190
  1022.8 0.9 fusion.2829
  1051.6 0.8 fusion.2766
  1079.6 0.8 fusion.733
  1080.5 0.8 convolution_negate_fusion.12
  1081.4 1.0 fusion.437
  1082.6 1.5 fusion.2808
  1112.2 0.8 fusion.2763
  1126.8 0.8 fusion.2481
  1144.5 0.8 convolution_negate_fusion.26
  1146.1 0.8 convolution_negate_fusion.11
  1147.8 0.9 convolution_negate_fusion.4
  1148.6 0.8 fusion.231
  1149.5 0.9 convolution_negate_fusion.1
  1150.4 0.9 fusion.100
  1151.3 1.0 convolution_negate_fusion
  1152.3 0.9 fusion.33
  1153.2 1.5 fusion.46
  1155.1 1.8 fusion.1
  1156.9 2.3 copy.272
  (1980 shorter events, 417.4 us)
Async XLA Ops:
  7.2 199.6 %all-reduce.376.cloned.1.call-start = ((), (), s32[]{:S(2)}) async-start(), calls=%async_computation | async-start | bytes 786432 | tf_op jit(solution)/shard_map/psum | solution.py:9
  685.1 222.4 %copy-start.27 = (f32[2,4]{1,0:T(2,128)}, f32[2,4]{1,0:T(2,128)S(1)}, u32[]{:S(2)}) copy-start(f32[2,4]{1,0:T(2,128)S(1)} %concatenate.8330) | copy-start | bytes 100
  685.3 222.2 %copy-start.28 = (f32[2,2]{1,0:T(2,128)}, f32[2,2]{1,0:T(2,128)S(1)}, u32[]{:S(2)}) copy-start(f32[2,2]{1,0:T(2,128)S(1)} %convolution_negate_fusion.183) | copy-start | bytes 52
  692.4 215.1 %copy-start.11 = (f32[4,8]{1,0:T(4,128)}, f32[4,8]{1,0:T(4,128)S(1)}, u32[]{:S(2)}) copy-start(f32[4,8]{1,0:T(4,128)S(1)} %concatenate.8342) | copy-start | bytes 388
  692.6 215.0 %copy-start.12 = (f32[4,4]{1,0:T(4,128)}, f32[4,4]{1,0:T(4,128)S(1)}, u32[]{:S(2)}) copy-start(f32[4,4]{1,0:T(4,128)S(1)} %convolution_negate_fusion.88) | copy-start | bytes 196
  706.8 200.7 %copy-start.14 = (f32[8,16]{1,0:T(8,128)}, f32[8,16]{1,0:T(8,128)S(1)}, u32[]{:S(2)}) copy-start(f32[8,16]{1,0:T(8,128)S(1)} %concatenate.8366) | copy-start | bytes 1540
  707.0 200.6 %copy-start.13 = (f32[8,8]{1,0:T(8,128)}, f32[8,8]{1,0:T(8,128)S(1)}, u32[]{:S(2)}) copy-start(f32[8,8]{1,0:T(8,128)S(1)} %convolution_negate_fusion.41) | copy-start | bytes 772
  735.5 172.1 %copy-start.8 = (f32[16,32]{1,0:T(8,128)}, f32[16,32]{1,0:T(8,128)S(1)}, u32[]{:S(2)}) copy-start(f32[16,32]{1,0:T(8,128)S(1)} %concatenate.8414) | copy-start | bytes 6148
  735.6 172.0 %copy-start.7 = (f32[16,16]{1,0:T(8,128)}, f32[16,16]{1,0:T(8,128)S(1)}, u32[]{:S(2)}) copy-start(f32[16,16]{1,0:T(8,128)S(1)} %convolution_negate_fusion.18) | copy-start | bytes 3076
  792.8 116.2 %copy-start.6 = (f32[32,64]{1,0:T(8,128)}, f32[32,64]{1,0:T(8,128)S(1)}, u32[]{:S(2)}) copy-start(f32[32,64]{1,0:T(8,128)S(1)} %concatenate.8510) | copy-start | bytes 24580
  916.1 145.2 %copy-start.29 = (f32[2,4]{1,0:T(2,128)}, f32[2,4]{1,0:T(2,128)S(1)}, u32[]{:S(2)}) copy-start(f32[2,4]{1,0:T(2,128)S(1)} %concatenate.8711) | copy-start | bytes 100
  916.2 145.1 %copy-start.39 = (f32[2,2]{1,0:T(2,128)}, f32[2,2]{1,0:T(2,128)S(1)}, u32[]{:S(2)}) copy-start(f32[2,2]{1,0:T(2,128)S(1)} %convolution_negate_fusion.151) | copy-start | bytes 52
  923.0 143.3 %copy-start.16 = (f32[4,8]{1,0:T(4,128)}, f32[4,8]{1,0:T(4,128)S(1)}, u32[]{:S(2)}) copy-start(f32[4,8]{1,0:T(4,128)S(1)} %concatenate.8723) | copy-start | bytes 388
  923.2 143.9 %copy-start.15 = (f32[4,4]{1,0:T(4,128)}, f32[4,4]{1,0:T(4,128)S(1)}, u32[]{:S(2)}) copy-start(f32[4,4]{1,0:T(4,128)S(1)} %convolution_negate_fusion.72) | copy-start | bytes 196
  937.1 142.4 %copy-start.36 = (f32[8,16]{1,0:T(8,128)}, f32[8,16]{1,0:T(8,128)S(1)}, u32[]{:S(2)}) copy-start(f32[8,16]{1,0:T(8,128)S(1)} %concatenate.8747) | copy-start | bytes 1540
  937.2 142.2 %copy-start.31 = (f32[8,8]{1,0:T(8,128)}, f32[8,8]{1,0:T(8,128)S(1)}, u32[]{:S(2)}) copy-start(f32[8,8]{1,0:T(8,128)S(1)} %convolution_negate_fusion.33) | copy-start | bytes 772
  965.3 142.3 %copy-start.19 = (f32[16,32]{1,0:T(8,128)}, f32[16,32]{1,0:T(8,128)S(1)}, u32[]{:S(2)}) copy-start(f32[16,32]{1,0:T(8,128)S(1)} %concatenate.8795) | copy-start | bytes 6148
  965.5 142.9 %copy-start.17 = (f32[16,16]{1,0:T(8,128)}, f32[16,16]{1,0:T(8,128)S(1)}, u32[]{:S(2)}) copy-start(f32[16,16]{1,0:T(8,128)S(1)} %convolution_negate_fusion.14) | copy-start | bytes 3076
  1022.1 118.4 %copy-start.10 = (f32[32,64]{1,0:T(8,128)}, f32[32,64]{1,0:T(8,128)S(1)}, u32[]{:S(2)}) copy-start(f32[32,64]{1,0:T(8,128)S(1)} %concatenate.8891) | copy-start | bytes 24580
  1022.2 118.2 %copy-start.9 = (f32[32,32]{1,0:T(8,128)}, f32[32,32]{1,0:T(8,128)S(1)}, u32[]{:S(2)}) copy-start(f32[32,32]{1,0:T(8,128)S(1)} %convolution_negate_fusion.5) | copy-start | bytes 12292
  1029.9 49.6 %copy-start.40 = (f32[2,2]{1,0:T(2,128)}, f32[2,2]{1,0:T(2,128)S(1)}, u32[]{:S(2)}) copy-start(f32[2,2]{1,0:T(2,128)S(1)} %convolution_negate_fusion.135) | copy-start | bytes 52
  1079.6 75.5 %copy-start.2 = (bf16[4096,128]{0,1:T(8,128)(2,1)S(1)}, bf16[4096,128]{0,1:T(8,128)(2,1)}, u32[]{:S(2)}) copy-start(bf16[4096,128]{0,1:T(8,128)(2,1)} %copy.270) | copy-start | bytes 3145732
  1080.5 60.0 %copy-start.20 = (f32[16,32]{1,0:T(8,128)}, f32[16,32]{1,0:T(8,128)S(1)}, u32[]{:S(2)}) copy-start(f32[16,32]{1,0:T(8,128)S(1)} %concatenate.8984) | copy-start | bytes 6148
  1090.4 50.1 %copy-start.41 = (f32[2,2]{1,0:T(2,128)}, f32[2,2]{1,0:T(2,128)S(1)}, u32[]{:S(2)}) copy-start(f32[2,2]{1,0:T(2,128)S(1)} %convolution_negate_fusion.127) | copy-start | bytes 52
  (23 other events, 438.7 us)
Sparse Core Ops, SparseCore 0:
  11.5 195.2 all-reduce.375
where the time goes:
time: 1190 us; the launch traced here: 1170 us
  between operations  530 us (45%)
  matrix products  206 us (17%)
  waiting for transfers between devices  194 us (16%)
  local copies, waits for them, and re-layouts  190 us (16%)
  other arithmetic  46.6 us (4%)
    dot_general x1005, matrix products, matmul(): return jnp.dot(left, right, precision=lax.Precision.HIGHEST)  202 us
    psum x1, waiting for transfers between devices, in_one(): running = lax.psum(vector, axis)  194 us
    slice x256, local copies, waits for them, and re-layouts, factor_inverse(): coupled = matmul(upper_inv.T, gram[:half, half:])  171 us
    concatenate x375, other arithmetic, factor_inverse(): jnp.concatenate([jnp.concatenate([upper_inv, corner], axis=1), jnp.concat...  35.6 us
  transfers between devices with their start and end apart: 1, of which 1 were waited for; matrix products, arithmetic and copies ran while one was open for 0% of the time, Pallas kernels for 0%

commit v1 on v0

v1 whole, which is shorter than its diff:
```python
import jax
import jax.numpy as jnp
from jax import lax
from jax.experimental import pallas as pl
from jax.experimental.pallas import tpu as pltpu
from jax.sharding import PartitionSpec as P

NB=32
def hdot(a,b,dims):
    return lax.dot_general(a,b,(dims,((),())),precision=lax.Precision.HIGHEST,preferred_element_type=jnp.float32)

def eliminate(m):
    nb=m.shape[0]
    rows=lax.broadcasted_iota(jnp.int32,m.shape,0)
    cols=lax.broadcasted_iota(jnp.int32,m.shape,1)
    for k in range(0,nb,2):
        r1=m[k:k+1,:]; r2=m[k+1:k+2,:]
        c1=jnp.broadcast_to(m[:,k:k+1],m.shape); c2=jnp.broadcast_to(m[:,k+1:k+2],m.shape)
        a=c1[k:k+1,:]; b=c2[k:k+1,:]; c=c2[k+1:k+2,:]
        inv=1.0/(a*c-b*b)
        r2n = r2-(b/a)*r1
        g1=(c*r1-b*r2)*inv
        g2=(a*r2-b*r1)*inv
        upd = m - c1*g1 - c2*g2
        m = jnp.where(rows>k+1, upd, jnp.where(rows==k+1, r2n, m))
    d=jnp.sum(jnp.where(rows==cols,m,0.0),axis=1,keepdims=True)
    m=m*lax.rsqrt(d)
    return jnp.where((cols>=nb)|(cols>=rows),m,0.0)

def chol_kernel(g_ref, r_ref, wt_ref, a_ref, b_ref):
    n=g_ref.shape[0]; nb=NB
    a_ref[...]=g_ref[...]
    eye=(lax.broadcasted_iota(jnp.int32,(nb,nb),0)==lax.broadcasted_iota(jnp.int32,(nb,nb),1)).astype(jnp.float32)
    r_ref[...]=jnp.zeros_like(r_ref)
    wt_ref[...]=jnp.zeros_like(wt_ref)
    b_ref[...]=jnp.zeros_like(b_ref)
    for i in range(n//nb):
        lo,hi=i*nb,(i+1)*nb
        m=jnp.concatenate([a_ref[lo:hi,lo:hi],eye],axis=1)
        m=eliminate(m)
        R=m[:,:nb]; Wt=m[:,nb:]
        r_ref[lo:hi,lo:hi]=R
        wt_ref[lo:hi,lo:hi]=Wt
        if lo>0:
            tb=hdot(Wt,b_ref[lo:hi,:lo],((1,),(0,)))
            wt_ref[lo:hi,:lo]=tb
        if hi<n:
            ta=hdot(Wt,a_ref[lo:hi,hi:],((1,),(0,)))
            r_ref[lo:hi,hi:]=ta
            a_ref[hi:,hi:]-=hdot(ta,ta,((0,),(0,)))
            b_ref[hi:,:hi]-=hdot(ta,wt_ref[lo:hi,:hi],((0,),(0,)))
def chol(g):
    n=g.shape[0]
    s=jax.ShapeDtypeStruct((n,n),jnp.float32)
    return pl.pallas_call(chol_kernel,out_shape=(s,s),scratch_shapes=[pltpu.VMEM((n,n),jnp.float32)]*2,name="chol")(g)


def exchange(parts):
    return lax.all_to_all(parts, "row", 0, 0, tiled=True)


def total(parts):
    mine = jnp.sum(exchange(parts), axis=0)
    return exchange(jnp.broadcast_to(mine[None], parts.shape))


def on_device(panel, slab):
    rows = lax.axis_size("row")
    scale = 1.0 / (panel.shape[0] * rows)
    contract = (((0,), (0,)), ((), ()))
    local_gram = lax.dot_general(panel, panel, contract, preferred_element_type=jnp.float32) * scale
    local_cross = lax.dot_general(panel, slab, contract, preferred_element_type=jnp.float32) * scale
    order, width = local_cross.shape
    tiles = local_gram.reshape(order // 8, 8, order // 128, 128).transpose(0, 2, 1, 3)
    tiles = total(tiles.reshape(rows, -1, 128)).reshape(tiles.shape)
    gram = tiles.transpose(0, 2, 1, 3).reshape(order, order)
    cross = total(local_cross.reshape(rows, -1, 128)).reshape(order, width)
    factor, inv_t = chol(gram)
    coupling = hdot(inv_t, cross, ((1,), (0,)))
    update = hdot(inv_t, coupling, ((0,), (0,))).astype(jnp.bfloat16)
    remainder = (
        slab.astype(jnp.float32) - jnp.dot(panel, update, preferred_element_type=jnp.float32)
    ).astype(jnp.bfloat16)
    share = factor.shape[1] // lax.axis_size("col")
    factor_part = lax.dynamic_slice_in_dim(factor, lax.axis_index("col") * share, share, 1)
    return (factor_part, coupling, remainder)


def solution(mesh):
    return jax.shard_map(
        on_device,
        mesh=mesh,
        in_specs=(P("row", None), P("row", "col")),
        out_specs=(P(None, "col"), P(None, "col"), P("row", "col")),
        check_vma=False,
    )
```

time: 1190 us -> 97.8 us (0.08); the launches traced: 1170 us -> 97.3 us
  between operations: 530 us -> 0.73 us
  matrix products: 206 us -> 7.57 us
  local copies, waits for them, and re-layouts: 190 us -> 8.3 us
  waiting for transfers between devices: 194 us -> 32.8 us
  other arithmetic: 46.6 us -> 0.15 us
  starting transfers between devices: 0.04 us -> 28.6 us
  Pallas kernels: 0 us -> 19.2 us
    dot_general x1005 -> x2, matrix products: 202 us -> 2.91 us  [hdot(): lax.dot_general(a, b, (dims, ((), ())), precision=lax.Precision.HIGHEST,...]
    psum x1 -> x0, waiting for transfers between devices: 194 us -> none  [in_one(): running = lax.psum(vector, axis)]
    slice x265 -> x0, local copies, waits for them, and re-layouts: 173 us -> none  [the longest x256 171 us: factor_inverse(): coupled = matmul(upper_inv.T, gram[:half, half:])]
    concatenate x503 -> x0, other arithmetic: 46.6 us -> none  [the longest x375 35.6 us: factor_inverse(): jnp.concatenate([jnp.concatenate([upper_inv, corner], axis=1), jnp.concat...]
    all_to_all x0 -> x4, waiting for transfers between devices: none -> 32.8 us  [exchange(): return lax.all_to_all(parts, 'row', 0, 0, tiled=True)]
    all_to_all x0 -> x4, starting transfers between devices: none -> 28.6 us  [exchange(): return lax.all_to_all(parts, 'row', 0, 0, tiled=True)]
    pallas_call x0 -> x1, Pallas kernels: none -> 19.2 us  [chol(): pl.pallas_call(chol_kernel, out_shape=(s, s), scratch_shapes=[pltpu.VMEM(...]
  transfers between devices with their start and end apart: 1 -> 4, of which waited for: 1 -> 3; matrix products, arithmetic and copies ran while one was open for 0% -> 5% of each run, Pallas kernels for 0% -> 20%
where the time goes in v1:
time: 97.8 us; the launch traced here: 97.3 us
  waiting for transfers between devices  32.8 us (34%)
  starting transfers between devices  28.6 us (29%)
  Pallas kernels  19.2 us (20%)
  local copies, waits for them, and re-layouts  8.3 us (8%)
  matrix products  7.57 us (8%)
    all_to_all x4, waiting for transfers between devices, exchange(): return lax.all_to_all(parts, 'row', 0, 0, tiled=True)  32.8 us
    all_to_all x4, starting transfers between devices, exchange(): return lax.all_to_all(parts, 'row', 0, 0, tiled=True)  28.6 us
    pallas_call x1, Pallas kernels, chol(): pl.pallas_call(chol_kernel, out_shape=(s, s), scratch_shapes=[pltpu.VMEM(...  19.2 us
    unnamed x13, local copies, waits for them, and re-layouts  5.87 us
    dot_general x2, matrix products, hdot(): lax.dot_general(a, b, (dims, ((), ())), precision=lax.Precision.HIGHEST,...  2.91 us
  transfers between devices with their start and end apart: 4, of which 3 were waited for; matrix products, arithmetic and copies ran while one was open for 5% of the time, Pallas kernels for 20%

profile of v1, /device:TPU:1, one launch (start us, length us, event | category | flops | bytes accessed | tf_op | source)
XLA Modules:
  0.0 97.3 jit_solution(11226605168180437293)
XLA Ops:
  0.6 0.0 copy-start
  0.6 1.6 %copy-done = bf16[4096,256]{1,0:T(8,128)(2,1)S(1)} copy-done((bf16[4096,256]{1,0:T(8,128)(2,1)S(1)}, bf16[4096,256]{1,0:T(8,128)(2,1)}, u32[]{:S(2)}) %copy-start) | copy-done | bytes 2097176
  2.2 1.4 %convolution_multiply_fusion = f32[256,256]{1,0:T(8,128)} fusion(bf16[4096,256]{1,0:T(8,128)(2,1)S(1)} %copy-done), kind=kOutput, calls=%fused_computation.3 | convolution fusion | flops 536936448 | bytes 2359296 | tf_op jit(solution)/shard_map/dot_general | solution.py:71
  3.7 11.6 %all-to-all-start = ((f32[64,8,128]{2,1,0:T(8,128)}), f32[64,8,128]{2,1,0:T(8,128)S(1)}, u32[]{:S(2)}, u32[]{:S(2)}) async-start(f32[64,8,128]{2,1,0:T(8,128)} %bitcast.30), calls=%async_computation | async-start | bytes 524288 | tf_op jit(solution)/shard_map/all_to_all | solution.py:59
  15.3 1.4 %convolution_multiply_fusion.1 = f32[256,128]{1,0:T(8,128)} fusion(bf16[4096,256]{1,0:T(8,128)(2,1)S(1)} %copy-done, bf16[4096,128]{1,0:T(8,128)(2,1)S(1)} %copy-done.1), kind=kOutput, calls=%fused_computation.4 | convolution fusion | flops 268468224 | bytes 3276800 | tf_op jit(solution)/shard_map/dot_general | solution.py:72
  16.7 10.6 %all-to-all-done = f32[64,8,128]{2,1,0:T(8,128)S(1)} async-done(((f32[64,8,128]{2,1,0:T(8,128)}), f32[64,8,128]{2,1,0:T(8,128)S(1)}, u32[]{:S(2)}, u32[]{:S(2)}) %all-to-all-start) | async-done | bytes 262176 | tf_op jit(solution)/shard_map/all_to_all | solution.py:59
  27.3 6.0 %all-to-all-start.2 = ((f32[64,4,128]{2,1,0:T(4,128)}), f32[64,4,128]{2,1,0:T(4,128)S(1)}, u32[]{:S(2)}, u32[]{:S(2)}) async-start(f32[64,4,128]{2,1,0:T(4,128)} %bitcast.6), calls=%async_computation.2 | async-start | bytes 262144 | tf_op jit(solution)/shard_map/all_to_all | solution.py:59
  33.3 0.1 reduce_sum.18
  33.4 10.3 %all-to-all-done.2 = f32[64,4,128]{2,1,0:T(4,128)S(1)} async-done(((f32[64,4,128]{2,1,0:T(4,128)}), f32[64,4,128]{2,1,0:T(4,128)S(1)}, u32[]{:S(2)}, u32[]{:S(2)}) %all-to-all-start.2) | async-done | bytes 131104 | tf_op jit(solution)/shard_map/all_to_all | solution.py:59
  43.7 0.7 broadcast_in_dim.4
  44.4 4.9 %all-to-all-start.1 = ((f32[64,8,128]{2,1,0:T(8,128)}), f32[64,8,128]{2,1,0:T(8,128)S(1)}, u32[]{:S(2)}, u32[]{:S(2)}) async-start(f32[64,8,128]{2,1,0:T(8,128)} %broadcast_in_dim.4), calls=%async_computation.1 | async-start | bytes 524288 | tf_op jit(solution)/shard_map/all_to_all | solution.py:59
  49.3 0.1 reduce_sum.19
  49.4 11.9 %all-to-all-done.1 = f32[64,8,128]{2,1,0:T(8,128)S(1)} async-done(((f32[64,8,128]{2,1,0:T(8,128)}), f32[64,8,128]{2,1,0:T(8,128)S(1)}, u32[]{:S(2)}, u32[]{:S(2)}) %all-to-all-start.1) | async-done | bytes 262176 | tf_op jit(solution)/shard_map/all_to_all | solution.py:59
  61.3 0.7 broadcast_in_dim.5
  62.0 6.0 %all-to-all-start.3 = ((f32[64,4,128]{2,1,0:T(4,128)}), f32[64,4,128]{2,1,0:T(4,128)S(1)}, u32[]{:S(2)}, u32[]{:S(2)}) async-start(f32[64,4,128]{2,1,0:T(4,128)} %broadcast_in_dim.5), calls=%async_computation.3 | async-start | bytes 262144 | tf_op jit(solution)/shard_map/all_to_all | solution.py:59
  68.1 1.3 %copy.5 = bf16[4096,128]{0,1:T(8,128)(2,1)} copy(bf16[4096,128]{1,0:T(8,128)(2,1)S(1)} %copy-done.1) | data formatting | bytes 2097152 | tf_op args[1]
  69.4 19.2 %chol.1 = (f32[256,256]{1,0:T(8,128)}, f32[256,256]{1,0:T(8,128)}) custom-call(f32[256,256]{1,0:T(8,128)} %bitcast.28), custom_call_target="tpu_custom_call" | custom-call | tf_op jit(solution)/shard_map/chol/pallas_call | solution.py:55
  88.6 1.0 %constant_dynamic-slice_fusion = f32[256,32]{1,0:T(8,128)S(1)} fusion(f32[256,256]{1,0:T(8,128)} %get-tuple-element.5, s32[]{:T(128)S(6)} %select_n.3), kind=kLoop, calls=%fused_computation.6 | loop fusion | bytes 65540 | tf_op jit(solution)/shard_map/dynamic_slice | solution.py:85
  89.6 0.7 copy.6
  90.3 1.3 %fusion.2 = f32[256,128]{1,0:T(8,128)S(1)} fusion(f32[256,256]{1,0:T(8,128)} %get-tuple-element.6, f32[256,128]{1,0:T(8,128)S(1)} %bitcast.29), kind=kOutput, calls=%fused_computation.7 | convolution fusion | flops 100663296 | bytes 524288 | tf_op jit(solution)/shard_map/dot_general | solution.py:10
  91.7 0.0 copy-start.4
  91.7 1.6 %convolution_convert_fusion = bf16[256,128]{1,0:T(8,128)(2,1)S(1)} fusion(f32[256,256]{1,0:T(8,128)} %get-tuple-element.6, f32[256,128]{1,0:T(8,128)S(1)} %fusion.2), kind=kOutput, calls=%fused_computation.5 | convolution fusion | flops 100696064 | bytes 458752 | tf_op jit(solution)/shard_map/dot_general | solution.py:10
  93.3 1.8 %fusion.1 = bf16[4096,128]{0,1:T(8,128)(2,1)} fusion(bf16[256,128]{1,0:T(8,128)(2,1)S(1)} %convolution_convert_fusion, bf16[4096,256]{1,0:T(8,128)(2,1)S(1)} %copy-done, bf16[4096,128]{0,1:T(8,128)(2,1)S(1)} %copy-done.2), kind=kOutput, calls=%fused_computation.2 | convolution fusion | flops 270008320 | bytes 4259840 | tf_op jit(solution)/shard_map/dot_general | solution.py:82
  95.1 2.3 %copy.7 = bf16[4096,128]{1,0:T(8,128)(2,1)} copy(bf16[4096,128]{0,1:T(8,128)(2,1)} %fusion.1) | data formatting | bytes 2097152
  (8 shorter events, 0.0 us)
Async XLA Ops:
  0.6 1.6 %copy-start = (bf16[4096,256]{1,0:T(8,128)(2,1)S(1)}, bf16[4096,256]{1,0:T(8,128)(2,1)}, u32[]{:S(2)}) copy-start(bf16[4096,256]{1,0:T(8,128)(2,1)} %param.2) | copy-start | bytes 6291460
  2.2 13.1 %copy-start.1 = (bf16[4096,128]{1,0:T(8,128)(2,1)S(1)}, bf16[4096,128]{1,0:T(8,128)(2,1)}, u32[]{:S(2)}) copy-start(bf16[4096,128]{1,0:T(8,128)(2,1)} %param.3) | copy-start | bytes 3145732
  3.7 23.6 %all-to-all-start = ((f32[64,8,128]{2,1,0:T(8,128)}), f32[64,8,128]{2,1,0:T(8,128)S(1)}, u32[]{:S(2)}, u32[]{:S(2)}) async-start(f32[64,8,128]{2,1,0:T(8,128)} %bitcast.30), calls=%async_computation | async-start | bytes 524288 | tf_op jit(solution)/shard_map/all_to_all | solution.py:59
  27.3 16.4 %all-to-all-start.2 = ((f32[64,4,128]{2,1,0:T(4,128)}), f32[64,4,128]{2,1,0:T(4,128)S(1)}, u32[]{:S(2)}, u32[]{:S(2)}) async-start(f32[64,4,128]{2,1,0:T(4,128)} %bitcast.6), calls=%async_computation.2 | async-start | bytes 262144 | tf_op jit(solution)/shard_map/all_to_all | solution.py:59
  44.4 16.9 %all-to-all-start.1 = ((f32[64,8,128]{2,1,0:T(8,128)}), f32[64,8,128]{2,1,0:T(8,128)S(1)}, u32[]{:S(2)}, u32[]{:S(2)}) async-start(f32[64,8,128]{2,1,0:T(8,128)} %broadcast_in_dim.4), calls=%async_computation.1 | async-start | bytes 524288 | tf_op jit(solution)/shard_map/all_to_all | solution.py:59
  61.3 8.1 %copy-start.3 = (f32[64,8,128]{2,1,0:T(8,128)}, f32[64,8,128]{2,1,0:T(8,128)S(1)}, u32[]{:S(2)}) copy-start(f32[64,8,128]{2,1,0:T(8,128)S(1)} %all-to-all-done.1) | copy-start | bytes 786436
  62.0 28.3 %all-to-all-start.3 = ((f32[64,4,128]{2,1,0:T(4,128)}), f32[64,4,128]{2,1,0:T(4,128)S(1)}, u32[]{:S(2)}, u32[]{:S(2)}) async-start(f32[64,4,128]{2,1,0:T(4,128)} %broadcast_in_dim.5), calls=%async_computation.3 | async-start | bytes 262144 | tf_op jit(solution)/shard_map/all_to_all | solution.py:59
  69.4 23.9 %copy-start.2 = (bf16[4096,128]{0,1:T(8,128)(2,1)S(1)}, bf16[4096,128]{0,1:T(8,128)(2,1)}, u32[]{:S(2)}) copy-start(bf16[4096,128]{0,1:T(8,128)(2,1)} %copy.5) | copy-start | bytes 3145732
  91.7 3.4 %copy-start.4 = (f32[256,128]{1,0:T(8,128)}, f32[256,128]{1,0:T(8,128)S(1)}, u32[]{:S(2)}) copy-start(f32[256,128]{1,0:T(8,128)S(1)} %fusion.2) | copy-start | bytes 393220

commit v2 on v0

v2 whole, which is shorter than its diff:
```python
import functools
import jax
import jax.numpy as jnp
from jax import lax
from jax.experimental import pallas as pl
from jax.experimental.pallas import tpu as pltpu
from jax.sharding import PartitionSpec as P

NB = 64


def hdot(a, b, dims):
    return lax.dot_general(
        a, b, (dims, ((), ())), precision=lax.Precision.HIGHEST, preferred_element_type=jnp.float32
    )


def row_of(x, s):
    return jnp.broadcast_to(x[s : s + 1, :], x.shape)


def eliminate(m, off, u_ref):
    count = m.shape[0] // 8
    g = [m[8 * i : 8 * i + 8, :] for i in range(count)]

    def lanes(x, j):
        return jnp.broadcast_to(x[:, off + j : off + j + 1], x.shape)

    c1 = [lanes(x, 0) for x in g]
    c2 = [lanes(x, 1) for x in g]
    for k in range(0, m.shape[0], 2):
        h, s = divmod(k, 8)
        r1, r2 = row_of(g[h], s), row_of(g[h], s + 1)
        a, b, c = row_of(c1[h], s), row_of(c2[h], s), row_of(c2[h], s + 1)
        ratio = b / a
        u_ref[k : k + 1, :] = (r1 * lax.rsqrt(a))[s : s + 1, :]
        u_ref[k + 1 : k + 2, :] = ((r2 - ratio * r1) * lax.rsqrt(c - b * ratio))[s + 1 : s + 2, :]
        if k + 2 == m.shape[0]:
            break
        inv = 1.0 / (a * c - b * b)
        p1, p2, p3 = c * inv, b * inv, a * inv
        h, t = divmod(k + 2, 8)
        v1, v2 = row_of(c1[h], t), row_of(c2[h], t)
        w1, w2 = row_of(c1[h], t + 1), row_of(c2[h], t + 1)
        x1, x2 = p1 * v1 - p2 * v2, p3 * v2 - p2 * v1
        y1, y2 = p1 * w1 - p2 * w2, p3 * w2 - p2 * w1
        g1, g2 = p1 * r1 - p2 * r2, p3 * r2 - p2 * r1
        for i in range(h, count):
            n1 = lanes(g[i], k + 2) - c1[i] * x1 - c2[i] * x2
            n2 = lanes(g[i], k + 3) - c1[i] * y1 - c2[i] * y2
            g[i] = g[i] - c1[i] * g1 - c2[i] * g2
            c1[i], c2[i] = n1, n2


def gather_kernel(scale, panel_ref, slab_ref, out_ref, gram, cross):
    step = pl.program_id(0)

    @pl.when(step == 0)
    def _():
        gram[...] = jnp.zeros_like(gram)
        cross[...] = jnp.zeros_like(cross)

    contract = (((0,), (0,)), ((), ()))
    panel = panel_ref[...]
    gram[...] += lax.dot_general(panel, panel, contract, preferred_element_type=jnp.float32)
    cross[...] += lax.dot_general(panel, slab_ref[...], contract, preferred_element_type=jnp.float32)

    @pl.when(step == pl.num_programs(0) - 1)
    def _():
        out_ref[:, 0:256] = gram[0:64, :] * scale
        out_ref[:, 256:384] = gram[64:128, 128:256] * scale
        out_ref[:, 384:512] = gram[128:192, 128:256] * scale
        lane = lax.broadcasted_iota(jnp.int32, (64, 128), 1)
        out_ref[:, 512:640] = jnp.where(lane >= 64, gram[64:128, 0:128], pltpu.roll(gram[192:256, 128:256], 64, 1)) * scale
        for i in range(4):
            out_ref[:, 640 + 128 * i : 768 + 128 * i] = cross[64 * i : 64 * i + 64, :] * scale


def local_sums(panel, slab, scale, chunk=1024):
    rows = panel.shape[0]
    return pl.pallas_call(
        functools.partial(gather_kernel, scale),
        grid=(rows // chunk,),
        in_specs=[pl.BlockSpec((chunk, 256), lambda i: (i, 0)), pl.BlockSpec((chunk, 128), lambda i: (i, 0))],
        out_specs=pl.BlockSpec((64, 1152), lambda i: (0, 0)),
        out_shape=jax.ShapeDtypeStruct((64, 1152), jnp.float32),
        scratch_shapes=[pltpu.VMEM((256, 256), jnp.float32), pltpu.VMEM((256, 128), jnp.float32)],
        name="sums",
    )(panel, slab)


CHUNKS = 8


def finish_kernel(which_ref, s_ref, panel_hbm, slab_hbm, l_ref, coup_ref, rem_hbm,
                  panel, slab, rem, x, t, r, u, sems):
    loads = [pltpu.make_async_copy(panel_hbm, panel, sems.at[0]), pltpu.make_async_copy(slab_hbm, slab, sems.at[1])]
    for load in loads:
        load.start()
    lane = lax.broadcasted_iota(jnp.int32, (64, 128), 1)
    sub = lax.broadcasted_iota(jnp.int32, (64, 128), 0)
    low = lane < 64
    eyes = [(lane == sub).astype(jnp.float32), (lane == sub + 64).astype(jnp.float32)]
    x[0:64, 0:256] = s_ref[:, 0:256]
    x[64:128, 128:256] = s_ref[:, 256:384]
    x[64:128, 0:128] = s_ref[:, 512:640]
    x[128:192, 128:256] = s_ref[:, 384:512]
    x[192:256, 128:256] = pltpu.roll(s_ref[:, 512:640], 64, 1)
    for i in range(4):
        x[64 * i : 64 * i + 64, 256:384] = s_ref[:, 640 + 128 * i : 768 + 128 * i]
        for j in range(2):
            x[64 * i : 64 * i + 64, 384 + 128 * j : 512 + 128 * j] = eyes[i % 2] if i // 2 == j else jnp.zeros((64, 128), jnp.float32)
    r[...] = jnp.zeros_like(r)
    update = jnp.zeros((256, 128), jnp.float32)
    for i in range(4):
        lo, hi = 64 * i, 64 * i + 64
        tile, off = lo // 128 * 128, lo % 128
        d = x[lo:hi, tile : tile + 128]
        m = jnp.where(low, d, eyes[1]) if off == 0 else jnp.where(low, eyes[0], d)
        eliminate(m, off, u)
        v = u[...]
        wt = v[:, 64 - off : 128 - off]
        start, end = hi // 128 * 128, 384 + (hi + 127) // 128 * 128
        ti = hdot(wt, x[lo:hi, start:end], ((1,), (0,)))
        t[lo:hi, start:end] = ti
        own = jnp.where((lane - off >= sub) & ((lane >= 64) == (off > 0)), v, 0.0)
        if off == 0:
            own = jnp.where(low, own, t[lo:hi, tile : tile + 128])
        r[lo:hi, tile : tile + 128] = own
        if tile == 0:
            r[lo:hi, 128:256] = t[lo:hi, 128:256]
        if hi < 256:
            down = hdot(ti[:, 0 : 256 - start], ti, ((0,), (0,)))
            x[hi:256, start:end] -= down[hi - start :, :]
        coup = t[lo:hi, 256:384]
        coup_ref[lo:hi, :] = coup
        wide = end - 384
        part = hdot(t[lo:hi, 384:end], coup, ((0,), (0,)))
        if wide < 256:
            update = update + jnp.concatenate([part, jnp.zeros((256 - wide, 128), jnp.float32)], axis=0)
        else:
            update = update + part
    update = update.astype(jnp.bfloat16)
    for load in loads:
        load.wait()
    step = panel.shape[0] // CHUNKS
    stores = []
    for i in range(CHUNKS):
        at = pl.ds(i * step, step)
        rem[at, :] = (
            slab[at, :].astype(jnp.float32) - jnp.dot(panel[at, :], update, preferred_element_type=jnp.float32)
        ).astype(jnp.bfloat16)
        store = pltpu.make_async_copy(rem.at[at, :], rem_hbm.at[at, :], sems.at[2 + i])
        store.start()
        stores.append(store)
    share = l_ref.shape[0]
    pick = lax.broadcasted_iota(jnp.int32, (share, 256), 1) == (
        lax.broadcasted_iota(jnp.int32, (share, 256), 0) + which_ref[0] * share
    )
    l_ref[...] = hdot(pick.astype(jnp.float32), r[...], ((1,), (1,)))
    for store in stores:
        store.wait()


def finish(which, sums, panel, slab, share):
    rows = panel.shape[0]
    vmem = pl.BlockSpec(memory_space=pltpu.VMEM)
    hbm = pl.BlockSpec(memory_space=pl.ANY)
    return pl.pallas_call(
        finish_kernel,
        in_specs=[pl.BlockSpec(memory_space=pltpu.SMEM), vmem, hbm, hbm],
        out_specs=(vmem, vmem, hbm),
        out_shape=(
            jax.ShapeDtypeStruct((share, 256), jnp.float32),
            jax.ShapeDtypeStruct((256, 128), jnp.float32),
            jax.ShapeDtypeStruct((rows, 128), jnp.bfloat16),
        ),
        scratch_shapes=[
            pltpu.VMEM((rows, 256), jnp.bfloat16),
            pltpu.VMEM((rows, 128), jnp.bfloat16),
            pltpu.VMEM((rows, 128), jnp.bfloat16),
            pltpu.VMEM((256, 640), jnp.float32),
            pltpu.VMEM((256, 640), jnp.float32),
            pltpu.VMEM((256, 256), jnp.float32),
            pltpu.VMEM((64, 128), jnp.float32),
            pltpu.SemaphoreType.DMA((2 + CHUNKS,)),
        ],
        compiler_params=pltpu.CompilerParams(vmem_limit_bytes=32 * 1024 * 1024),
        name="finish",
    )(which, sums, panel, slab)


def exchange(parts):
    return lax.all_to_all(parts, "row", 0, 0, tiled=True)


def on_device(panel, slab):
    rows = lax.axis_size("row")
    parts = exchange(local_sums(panel, slab, 1.0 / (panel.shape[0] * rows)))
    mine = jnp.sum(parts, axis=0, keepdims=True)
    sums = exchange(jnp.broadcast_to(mine, parts.shape))
    share = panel.shape[1] // lax.axis_size("col")
    which = lax.axis_index("col").astype(jnp.int32).reshape(1)
    lower, coupling, remainder = finish(which, sums, panel, slab, share)
    return (lower.T, coupling, remainder)


def solution(mesh):
    return jax.shard_map(
        on_device,
        mesh=mesh,
        in_specs=(P("row", None), P("row", "col")),
        out_specs=(P(None, "col"), P(None, "col"), P("row", "col")),
        check_vma=False,
    )
```

time: 1190 us -> 62.5 us (0.05); the launches traced: 1170 us -> 62.2 us
  between operations: 530 us -> 0.68 us
  matrix products: 206 us -> 0 us
  local copies, waits for them, and re-layouts: 190 us -> 2.31 us
  waiting for transfers between devices: 194 us -> 12.7 us
  other arithmetic: 46.6 us -> 0.2 us
  blocking collectives: 0 us -> 24.1 us
  Pallas kernels: 0 us -> 16.2 us
    dot_general x1008 -> x0, matrix products: 206 us -> none  [the longest x1005 202 us: matmul(): return jnp.dot(left, right, precision=lax.Precision.HIGHEST)]
    psum x1 -> x0, waiting for transfers between devices: 194 us -> none  [in_one(): running = lax.psum(vector, axis)]
    slice x265 -> x0, local copies, waits for them, and re-layouts: 173 us -> none  [the longest x256 171 us: factor_inverse(): coupled = matmul(upper_inv.T, gram[:half, half:])]
    concatenate x503 -> x0, other arithmetic: 46.6 us -> none  [the longest x375 35.6 us: factor_inverse(): jnp.concatenate([jnp.concatenate([upper_inv, corner], axis=1), jnp.concat...]
    all_to_all x0 -> x1, blocking collectives: none -> 24.1 us  [exchange(): return lax.all_to_all(parts, 'row', 0, 0, tiled=True)]
    pallas_call x0 -> x2, Pallas kernels: none -> 16.2 us  [the longest x1 11.6 us: finish(): pl.pallas_call(finish_kernel, in_specs=[pl.BlockSpec(memory_space=pltpu.S...]
    all_to_all x0 -> x1, waiting for transfers between devices: none -> 12.7 us  [exchange(): return lax.all_to_all(parts, 'row', 0, 0, tiled=True)]
where the time goes in v2:
time: 62.5 us; the launch traced here: 62.2 us
  blocking collectives  24.1 us (39%)
  Pallas kernels  16.2 us (26%)
  waiting for transfers between devices  12.7 us (20%)
  starting transfers between devices  6.07 us (10%)
  local copies, waits for them, and re-layouts  2.31 us (4%)
  between operations  0.68 us (1%)
    all_to_all x1, blocking collectives, exchange(): return lax.all_to_all(parts, 'row', 0, 0, tiled=True)  24.1 us
    all_to_all x1, waiting for transfers between devices, exchange(): return lax.all_to_all(parts, 'row', 0, 0, tiled=True)  12.7 us
    pallas_call x1, Pallas kernels, finish(): pl.pallas_call(finish_kernel, in_specs=[pl.BlockSpec(memory_space=pltpu.S...  11.6 us
    all_to_all x1, starting transfers between devices, exchange(): return lax.all_to_all(parts, 'row', 0, 0, tiled=True)  6.07 us
    pallas_call x1, Pallas kernels, local_sums(): pl.pallas_call(functools.partial(gather_kernel, scale), grid=(rows // chu...  4.63 us
    all_to_all x1, local copies, waits for them, and re-layouts, exchange(): return lax.all_to_all(parts, 'row', 0, 0, tiled=True)  1.41 us
  transfers between devices with their start and end apart: 1, of which 1 were waited for; matrix products, arithmetic and copies ran while one was open for 0% of the time, Pallas kernels for 0%

profile of v2, /device:TPU:1, one launch (start us, length us, event | category | flops | bytes accessed | tf_op | source)
XLA Modules:
  0.0 62.2 jit_solution(11578265836724979156)
XLA Ops:
  0.6 0.0 copy-start.1
  0.6 4.6 %sums.1 = f32[64,1152]{1,0:T(8,128)} custom-call(bf16[4096,256]{1,0:T(8,128)(2,1)} %panel_hbm.1, bf16[4096,128]{1,0:T(8,128)(2,1)} %slab_hbm.1), custom_call_target="tpu_custom_call" | custom-call | tf_op jit(solution)/shard_map/sums/pallas_call | solution.py:81
  5.3 0.0 copy-start
  5.3 1.4 %copy.5 = f32[64,1,1152]{2,1,0:T(1,128)S(1)} copy(f32[64,1,1152]{2,0,1:T(8,128)} %bitcast.7) | data formatting | bytes 589824 | tf_op jit(solution)/shard_map/all_to_all | solution.py:194
  6.7 24.1 %all_to_all.17 = f32[64,1,1152]{2,1,0:T(1,128)S(1)} all-to-all(f32[64,1,1152]{2,1,0:T(1,128)S(1)} %copy.5), channel_id=1, replica_groups=mesh['row'=64,'col'=8] {'row'}, dimensions={0} | all-to-all | bytes 589824 | tf_op jit(solution)/shard_map/all_to_all | solution.py:194
  30.8 0.2 reduce_sum.9
  31.0 0.9 %broadcast_in_dim.2 = f32[64,1,1152]{2,1,0:T(1,128)} broadcast(f32[1152]{0:T(1024)S(1)} %reduce_sum.9), dimensions={2} | broadcast | bytes 299520 | tf_op jit(solution)/shard_map/broadcast_in_dim | solution.py:201
  31.8 6.1 %all-to-all-start.1 = ((f32[64,1,1152]{2,1,0:T(1,128)}), f32[64,1,1152]{2,1,0:T(1,128)S(1)}, u32[]{:S(2)}, u32[]{:S(2)}) async-start(f32[64,1,1152]{2,1,0:T(1,128)} %broadcast_in_dim.2), calls=%async_computation.1 | async-start | bytes 589824 | tf_op jit(solution)/shard_map/all_to_all | solution.py:194
  37.9 12.7 %all-to-all-done.1 = f32[64,1,1152]{2,1,0:T(1,128)S(1)} async-done(((f32[64,1,1152]{2,1,0:T(1,128)}), f32[64,1,1152]{2,1,0:T(1,128)S(1)}, u32[]{:S(2)}, u32[]{:S(2)}) %all-to-all-start.1) | async-done | bytes 294944 | tf_op jit(solution)/shard_map/all_to_all | solution.py:194
  50.6 0.0 copy-done.1
  50.6 0.0 copy-done
  50.6 11.6 %finish.1 = (f32[32,256]{1,0:T(8,128)}, f32[256,128]{1,0:T(8,128)}, bf16[4096,128]{1,0:T(8,128)(2,1)}) custom-call(s32[1]{0:T(128)} %bitcast.which_ref, f32[64,1152]{1,0:T(8,128)S(1)} %bitcast.6, bf16[4096,256]{1,0:T(8,128)(2,1)S(1)} %copy-done, bf16[4096,128]{1,0:T(8,128)(2,1)S(1)} %copy-done.1), custom_call_target="tpu_custom_call" | custom-call | tf_op jit(solution)/shard_map/finish/pallas_call | solution.py:169
  (1 shorter events, 0.0 us)
Async XLA Ops:
  0.6 50.0 %copy-start.1 = (bf16[4096,128]{1,0:T(8,128)(2,1)S(1)}, bf16[4096,128]{1,0:T(8,128)(2,1)}, u32[]{:S(2)}) copy-start(bf16[4096,128]{1,0:T(8,128)(2,1)} %slab_hbm.1) | copy-start | bytes 3145732
  5.3 45.3 %copy-start = (bf16[4096,256]{1,0:T(8,128)(2,1)S(1)}, bf16[4096,256]{1,0:T(8,128)(2,1)}, u32[]{:S(2)}) copy-start(bf16[4096,256]{1,0:T(8,128)(2,1)} %panel_hbm.1) | copy-start | bytes 6291460
  31.8 18.7 %all-to-all-start.1 = ((f32[64,1,1152]{2,1,0:T(1,128)}), f32[64,1,1152]{2,1,0:T(1,128)S(1)}, u32[]{:S(2)}, u32[]{:S(2)}) async-start(f32[64,1,1152]{2,1,0:T(1,128)} %broadcast_in_dim.2), calls=%async_computation.1 | async-start | bytes 589824 | tf_op jit(solution)/shard_map/all_to_all | solution.py:194

commit v3 on v2

v3 whole, which is shorter than its diff:
```python
import functools
import jax
import jax.numpy as jnp
from jax import lax
from jax.experimental import pallas as pl
from jax.experimental.pallas import tpu as pltpu
from jax.sharding import PartitionSpec as P

NB = 64


def hdot(a, b, dims):
    return lax.dot_general(
        a, b, (dims, ((), ())), precision=lax.Precision.HIGHEST, preferred_element_type=jnp.float32
    )


def row_of(x, s):
    return jnp.broadcast_to(x[s : s + 1, :], x.shape)


def eliminate(m, off, u_ref):
    count = m.shape[0] // 8
    g = [m[8 * i : 8 * i + 8, :] for i in range(count)]

    def lanes(x, j):
        return jnp.broadcast_to(x[:, off + j : off + j + 1], x.shape)

    ahead = [lanes(g[0], j) for j in range(8)]
    for h in range(count):
        cols = {h: ahead}
        if h + 1 < count:
            cols[h + 1] = [lanes(g[h + 1], 8 * h + j) for j in range(8)]
            ahead = [lanes(g[h + 1], 8 * h + 8 + j) for j in range(8)]
        rows = [row_of(g[h], r) for r in range(8)]
        invs, mults, scaled = [], [], []
        for j in range(8):
            pivot = row_of(cols[h][j], j)
            inv = 1.0 / pivot
            mult = {r: row_of(cols[h][j], r) * inv for r in range(j + 1, 8)}
            for r in range(j + 1, 8):
                cols[h][r] = cols[h][r] - cols[h][j] * mult[r]
            for r in range(j + 1, 8):
                rows[r] = rows[r] - mult[r] * rows[j]
            if h + 1 < count:
                for r in range(j + 1, 8):
                    cols[h + 1][r] = cols[h + 1][r] - cols[h + 1][j] * mult[r]
                ahead = [x - cols[h + 1][j] * (row_of(cols[h + 1][j], n) * inv) for n, x in enumerate(ahead)]
            scaled.append(rows[j] * inv)
            mults.append(mult)
            u_ref[8 * h + j : 8 * h + j + 1, :] = (rows[j] * lax.rsqrt(pivot))[j : j + 1, :]
        for i in range(h + 1, count):
            if i > h + 1:
                cols[i] = [lanes(g[i], 8 * h + j) for j in range(8)]
                for j in range(8):
                    for r in range(j + 1, 8):
                        cols[i][r] = cols[i][r] - cols[i][j] * mults[j][r]
            terms = [cols[i][j] * scaled[j] for j in range(8)]
            while len(terms) > 1:
                terms = [terms[n] + terms[n + 1] for n in range(0, len(terms), 2)]
            g[i] = g[i] - terms[0]


def gather_kernel(scale, groups, panel_hbm, slab_hbm, out, panel, slab, acc, sems):
    pieces = sum(groups)
    step = panel.shape[0] // pieces
    copies = []
    for i in range(pieces):
        at = pl.ds(i * step, step)
        pair = (
            pltpu.make_async_copy(panel_hbm.at[at, :], panel.at[at, :], sems.at[2 * i]),
            pltpu.make_async_copy(slab_hbm.at[at, :], slab.at[at, :], sems.at[2 * i + 1]),
        )
        for copy in pair:
            copy.start()
        copies.append(pair)
    contract = (((0,), (0,)), ((), ()))
    first = 0
    for n, size in enumerate(groups):
        for pair in copies[first : first + size]:
            for copy in pair:
                copy.wait()
        lo, hi = first * step, (first + size) * step
        first += size
        left = panel[lo:hi, :]
        right = jnp.concatenate([left, slab[lo:hi, :]], axis=1)
        top = lax.dot_general(left[:, :128], right, contract, preferred_element_type=jnp.float32)
        low = lax.dot_general(left[:, 128:], right[:, 128:], contract, preferred_element_type=jnp.float32)
        if n == 0:
            acc[0:128, :] = top
            acc[128:256, 128:384] = low
        else:
            acc[0:128, :] += top
            acc[128:256, 128:384] += low
    out[:, 0, 0:256] = acc[0:64, 0:256] * scale
    out[:, 0, 256:384] = acc[64:128, 128:256] * scale
    out[:, 0, 384:512] = acc[128:192, 128:256] * scale
    lane = lax.broadcasted_iota(jnp.int32, (64, 128), 1)
    out[:, 0, 512:640] = jnp.where(lane >= 64, acc[64:128, 0:128], pltpu.roll(acc[192:256, 128:256], 64, 1)) * scale
    for i in range(4):
        out[:, 0, 640 + 128 * i : 768 + 128 * i] = acc[64 * i : 64 * i + 64, 256:384] * scale


def local_sums(panel, slab, scale, groups=(2, 2)):
    rows = panel.shape[0]
    return pl.pallas_call(
        functools.partial(gather_kernel, scale, groups),
        in_specs=[pl.BlockSpec(memory_space=pl.ANY)] * 2,
        out_specs=pl.BlockSpec(memory_space=pltpu.VMEM),
        out_shape=jax.ShapeDtypeStruct((64, 1, 1152), jnp.float32),
        scratch_shapes=[
            pltpu.VMEM((rows, 256), jnp.bfloat16),
            pltpu.VMEM((rows, 128), jnp.bfloat16),
            pltpu.VMEM((256, 384), jnp.float32),
            pltpu.SemaphoreType.DMA((2 * sum(groups),)),
        ],
        compiler_params=pltpu.CompilerParams(vmem_limit_bytes=60 * 1024 * 1024),
        name="sums",
    )(panel, slab)


CHUNKS = 8


def finish_kernel(s_ref, panel_hbm, slab_hbm, l_ref, coup_ref, rem_hbm,
                  panel, slab, rem, x, t, r, u, sems):
    loads = [pltpu.make_async_copy(panel_hbm, panel, sems.at[0]), pltpu.make_async_copy(slab_hbm, slab, sems.at[1])]
    for load in loads:
        load.start()
    lane = lax.broadcasted_iota(jnp.int32, (64, 128), 1)
    sub = lax.broadcasted_iota(jnp.int32, (64, 128), 0)
    low = lane < 64
    eyes = [(lane == sub).astype(jnp.float32), (lane == sub + 64).astype(jnp.float32)]
    x[0:64, 0:256] = s_ref[:, 0:256]
    x[64:128, 128:256] = s_ref[:, 256:384]
    x[64:128, 0:128] = s_ref[:, 512:640]
    x[128:192, 128:256] = s_ref[:, 384:512]
    x[192:256, 128:256] = pltpu.roll(s_ref[:, 512:640], 64, 1)
    for i in range(4):
        x[64 * i : 64 * i + 64, 256:384] = s_ref[:, 640 + 128 * i : 768 + 128 * i]
        for j in range(2):
            x[64 * i : 64 * i + 64, 384 + 128 * j : 512 + 128 * j] = eyes[i % 2] if i // 2 == j else jnp.zeros((64, 128), jnp.float32)
    r[...] = jnp.zeros_like(r)
    def rest(i, v, wt):
        lo, hi = 64 * i, 64 * i + 64
        tile, off = lo // 128 * 128, lo % 128
        start, end = hi // 128 * 128, 384 + (hi + 127) // 128 * 128
        ti = hdot(wt, x[lo:hi, start:end], ((1,), (0,)))
        t[lo:hi, start:end] = ti
        own = jnp.where((lane - off >= sub) & ((lane >= 64) == (off > 0)), v, 0.0)
        if off == 0:
            own = jnp.where(low, own, t[lo:hi, tile : tile + 128])
        r[lo:hi, tile : tile + 128] = own
        if tile == 0:
            r[lo:hi, 128:256] = t[lo:hi, 128:256]
        if hi < 256:
            down = hdot(ti[:, 0 : 256 - start], ti, ((0,), (0,)))
            x[hi:256, start:end] -= down[hi - start :, :]
        coup = t[lo:hi, 256:384]
        coup_ref[lo:hi, :] = coup
        wide = end - 384
        part = hdot(t[lo:hi, 384:end], coup, ((0,), (0,)))
        if wide < 256:
            part = jnp.concatenate([part, jnp.zeros((256 - wide, 128), jnp.float32)], axis=0)
        return part

    def next_block(i, wt):
        lo, hi = 64 * i, 64 * i + 64
        tile, off = hi // 128 * 128, hi % 128
        ti = hdot(wt, x[lo:hi, tile : tile + 128], ((1,), (0,)))
        down = hdot(ti, ti, ((0,), (0,)))
        return x[hi : hi + 64, tile : tile + 128] - down[off : off + 64, :]

    update = None
    d = x[0:64, 0:128]
    held = None
    for i in range(4):
        m = jnp.where(low, d, eyes[1]) if i % 2 == 0 else jnp.where(low, eyes[0], d)
        eliminate(m, 64 * (i % 2), u.at[i])
        v = u[i]
        wt = v[:, 64:128] if i % 2 == 0 else v[:, 0:64]
        if held is not None:
            part = rest(*held)
            update = part if update is None else update + part
        if i < 3:
            d = next_block(i, wt)
        held = (i, v, wt)
    update = update + rest(*held)
    update = update.astype(jnp.bfloat16)
    for load in loads:
        load.wait()
    step = panel.shape[0] // CHUNKS
    stores = []
    for i in range(CHUNKS):
        at = pl.ds(i * step, step)
        rem[at, :] = (
            slab[at, :].astype(jnp.float32) - jnp.dot(panel[at, :], update, preferred_element_type=jnp.float32)
        ).astype(jnp.bfloat16)
        store = pltpu.make_async_copy(rem.at[at, :], rem_hbm.at[at, :], sems.at[2 + i])
        store.start()
        stores.append(store)
    share = l_ref.shape[0]
    pick = lax.broadcasted_iota(jnp.int32, (share, 256), 1) == (
        lax.broadcasted_iota(jnp.int32, (share, 256), 0) + lax.axis_index("col") * share
    )
    l_ref[...] = hdot(pick.astype(jnp.float32), r[...], ((1,), (1,)))
    for store in stores:
        store.wait()


def finish(sums, panel, slab, share):
    rows = panel.shape[0]
    vmem = pl.BlockSpec(memory_space=pltpu.VMEM)
    hbm = pl.BlockSpec(memory_space=pl.ANY)
    return pl.pallas_call(
        finish_kernel,
        in_specs=[vmem, hbm, hbm],
        out_specs=(vmem, vmem, hbm),
        out_shape=(
            jax.ShapeDtypeStruct((share, 256), jnp.float32),
            jax.ShapeDtypeStruct((256, 128), jnp.float32),
            jax.ShapeDtypeStruct((rows, 128), jnp.bfloat16),
        ),
        scratch_shapes=[
            pltpu.VMEM((rows, 256), jnp.bfloat16),
            pltpu.VMEM((rows, 128), jnp.bfloat16),
            pltpu.VMEM((rows, 128), jnp.bfloat16),
            pltpu.VMEM((256, 640), jnp.float32),
            pltpu.VMEM((256, 640), jnp.float32),
            pltpu.VMEM((256, 256), jnp.float32),
            pltpu.VMEM((4, 64, 128), jnp.float32),
            pltpu.SemaphoreType.DMA((2 + CHUNKS,)),
        ],
        compiler_params=pltpu.CompilerParams(vmem_limit_bytes=32 * 1024 * 1024),
        name="finish",
    )(sums, panel, slab)


def exchange(parts):
    return lax.all_to_all(parts, "row", 0, 0, tiled=True)


def on_device(panel, slab):
    rows = lax.axis_size("row")
    parts = exchange(local_sums(panel, slab, 1.0 / (panel.shape[0] * rows)))
    mine = jnp.sum(parts, axis=0, keepdims=True)
    sums = exchange(jnp.broadcast_to(mine, parts.shape))
    share = panel.shape[1] // lax.axis_size("col")
    lower, coupling, remainder = finish(sums.reshape(rows, -1), panel, slab, share)
    return (lower.T, coupling, remainder)


def solution(mesh):
    return jax.shard_map(
        on_device,
        mesh=mesh,
        in_specs=(P("row", None), P("row", "col")),
        out_specs=(P(None, "col"), P(None, "col"), P("row", "col")),
        check_vma=False,
    )
```

time: 62.5 us -> 57.8 us (0.925)
  blocking collectives: 24.1 us -> 42.8 us
  waiting for transfers between devices: 12.7 us -> 0 us
  starting transfers between devices: 6.07 us -> 0 us
  Pallas kernels: 16.2 us -> 13.7 us
  local copies, waits for them, and re-layouts: 2.31 us -> 0.18 us
    all_to_all x1 -> x2, blocking collectives: 24.1 us -> 42.8 us  [exchange(): return lax.all_to_all(parts, 'row', 0, 0, tiled=True)]
    all_to_all x1 -> x0, waiting for transfers between devices: 12.7 us -> none  [exchange(): return lax.all_to_all(parts, 'row', 0, 0, tiled=True)]
    all_to_all x1 -> x0, starting transfers between devices: 6.07 us -> none  [exchange(): return lax.all_to_all(parts, 'row', 0, 0, tiled=True)]
    pallas_call x2, Pallas kernels: 16.2 us -> 13.7 us  [the longest x1 10.1 us: finish(): pl.pallas_call(finish_kernel, in_specs=[vmem, hbm, hbm], out_specs=(vmem,...]
    all_to_all x1 -> x0, local copies, waits for them, and re-layouts: 1.41 us -> none  [exchange(): return lax.all_to_all(parts, 'row', 0, 0, tiled=True)]
    broadcast_in_dim x1, local copies, waits for them, and re-layouts: 0.87 us -> 0.15 us  [on_device(): sums = exchange(jnp.broadcast_to(mine, parts.shape))]
  transfers between devices with their start and end apart: 1 -> 0, of which waited for: 1 -> 0; matrix products, arithmetic and copies ran while one was open for 0% -> 0% of each run, Pallas kernels for 0% -> 0%
where the time goes in v3:
time: 57.8 us; the launch traced here: 57.6 us
  blocking collectives  42.8 us (74%)
  Pallas kernels  13.7 us (24%)
  between operations  0.68 us (1%)
    all_to_all x2, blocking collectives, exchange(): return lax.all_to_all(parts, 'row', 0, 0, tiled=True)  42.8 us
    pallas_call x1, Pallas kernels, finish(): pl.pallas_call(finish_kernel, in_specs=[vmem, hbm, hbm], out_specs=(vmem,...  10.1 us
    pallas_call x1, Pallas kernels, local_sums(): pl.pallas_call(functools.partial(gather_kernel, scale, groups), in_specs=...  3.59 us

profile of v3, /device:TPU:1, one launch (start us, length us, event | category | flops | bytes accessed | tf_op | source)
XLA Modules:
  0.0 57.6 jit_solution(13439055819116045349)
XLA Ops:
  0.6 0.0 copy-start.1
  0.6 0.0 copy-start
  0.6 3.6 %sums.1 = f32[64,1,1152]{2,1,0:T(1,128)} custom-call(bf16[4096,256]{1,0:T(8,128)(2,1)} %panel_hbm.3, bf16[4096,128]{1,0:T(8,128)(2,1)} %slab_hbm.3), custom_call_target="tpu_custom_call" | custom-call | tf_op jit(solution)/shard_map/sums/pallas_call | solution.py:106
  4.2 24.3 %all_to_all.10 = f32[64,1,1152]{2,1,0:T(1,128)S(1)} all-to-all(f32[64,1,1152]{2,1,0:T(1,128)} %sums.1), channel_id=1, replica_groups=mesh['row'=64,'col'=8] {'row'}, dimensions={0} | all-to-all | bytes 589824 | tf_op jit(solution)/shard_map/all_to_all | solution.py:240
  28.5 0.2 reduce_sum.9
  28.7 0.2 broadcast_in_dim.2
  28.9 18.5 %all_to_all.11 = f32[64,1,1152]{2,1,0:T(1,128)S(1)} all-to-all(f32[64,1,1152]{2,1,0:T(1,128)S(1)} %broadcast_in_dim.2), channel_id=1, replica_groups=mesh['row'=64,'col'=8] {'row'}, dimensions={0} | all-to-all | bytes 589824 | tf_op jit(solution)/shard_map/all_to_all | solution.py:240
  47.4 0.0 copy-done.1
  47.5 0.0 copy-done
  47.5 10.1 %finish.1 = (f32[32,256]{1,0:T(8,128)}, f32[256,128]{1,0:T(8,128)}, bf16[4096,128]{1,0:T(8,128)(2,1)}) custom-call(f32[64,1152]{1,0:T(8,128)S(1)} %bitcast.4, bf16[4096,256]{1,0:T(8,128)(2,1)S(1)} %copy-done, bf16[4096,128]{1,0:T(8,128)(2,1)S(1)} %copy-done.1), custom_call_target="tpu_custom_call" | custom-call | tf_op jit(solution)/shard_map/finish/pallas_call | solution.py:215
  (1 shorter events, 0.0 us)
Async XLA Ops:
  0.6 46.8 %copy-start.1 = (bf16[4096,128]{1,0:T(8,128)(2,1)S(1)}, bf16[4096,128]{1,0:T(8,128)(2,1)}, u32[]{:S(2)}) copy-start(bf16[4096,128]{1,0:T(8,128)(2,1)} %slab_hbm.3) | copy-start | bytes 3145732
  0.6 46.8 %copy-start = (bf16[4096,256]{1,0:T(8,128)(2,1)S(1)}, bf16[4096,256]{1,0:T(8,128)(2,1)}, u32[]{:S(2)}) copy-start(bf16[4096,256]{1,0:T(8,128)(2,1)} %panel_hbm.3) | copy-start | bytes 6291460

commit v4 on v3

--- a/solution.py
+++ b/solution.py
@@ -28,34 +28,44 @@
 
     ahead = [lanes(g[0], j) for j in range(8)]
     for h in range(count):
-        cols = {h: ahead}
+        near = {h: ahead}
         if h + 1 < count:
-            cols[h + 1] = [lanes(g[h + 1], 8 * h + j) for j in range(8)]
+            near[h + 1] = [lanes(g[h + 1], 8 * h + j) for j in range(8)]
             ahead = [lanes(g[h + 1], 8 * h + 8 + j) for j in range(8)]
-        rows = [row_of(g[h], r) for r in range(8)]
-        invs, mults, scaled = [], [], []
+        mine = near[h]
+        block = g[h]
+        rows, invs, entries, shares = [], [], [], []
         for j in range(8):
-            pivot = row_of(cols[h][j], j)
+            pivot = row_of(mine[j], j)
             inv = 1.0 / pivot
-            mult = {r: row_of(cols[h][j], r) * inv for r in range(j + 1, 8)}
+            entry = {r: row_of(mine[j], r) for r in range(j + 1, 8)}
+            row = row_of(block, j)
+            share = mine[j] * inv
             for r in range(j + 1, 8):
-                cols[h][r] = cols[h][r] - cols[h][j] * mult[r]
-            for r in range(j + 1, 8):
-                rows[r] = rows[r] - mult[r] * rows[j]
+                mine[r] = mine[r] - share * entry[r]
+            if j < 7:
+                block = block - share * row
             if h + 1 < count:
+                below = near[h + 1]
+                part = below[j] * inv
                 for r in range(j + 1, 8):
-                    cols[h + 1][r] = cols[h + 1][r] - cols[h + 1][j] * mult[r]
-                ahead = [x - cols[h + 1][j] * (row_of(cols[h + 1][j], n) * inv) for n, x in enumerate(ahead)]
-            scaled.append(rows[j] * inv)
-            mults.append(mult)
-            u_ref[8 * h + j : 8 * h + j + 1, :] = (rows[j] * lax.rsqrt(pivot))[j : j + 1, :]
+                    below[r] = below[r] - part * entry[r]
+                ahead = [x - below[j] * row_of(part, n) for n, x in enumerate(ahead)]
+                shares.append(part)
+            u_ref[8 * h + j : 8 * h + j + 1, :] = (row * lax.rsqrt(pivot))[j : j + 1, :]
+            rows.append(row)
+            invs.append(inv)
+            entries.append(entry)
         for i in range(h + 1, count):
             if i > h + 1:
-                cols[i] = [lanes(g[i], 8 * h + j) for j in range(8)]
+                far = [lanes(g[i], 8 * h + j) for j in range(8)]
+                shares = []
                 for j in range(8):
+                    part = far[j] * invs[j]
                     for r in range(j + 1, 8):
-                        cols[i][r] = cols[i][r] - cols[i][j] * mults[j][r]
-            terms = [cols[i][j] * scaled[j] for j in range(8)]
+                        far[r] = far[r] - part * entries[j][r]
+                    shares.append(part)
+            terms = [share * row for share, row in zip(shares, rows)]
             while len(terms) > 1:
                 terms = [terms[n] + terms[n + 1] for n in range(0, len(terms), 2)]
             g[i] = g[i] - terms[0]
@@ -119,14 +129,11 @@
     )(panel, slab)
 
 
-CHUNKS = 8
-
-
-def finish_kernel(s_ref, panel_hbm, slab_hbm, l_ref, coup_ref, rem_hbm,
-                  panel, slab, rem, x, t, r, u, sems):
-    loads = [pltpu.make_async_copy(panel_hbm, panel, sems.at[0]), pltpu.make_async_copy(slab_hbm, slab, sems.at[1])]
-    for load in loads:
-        load.start()
+CHUNKS = 4
+
+
+def finish_kernel(s_ref, panel, slab, l_ref, coup_ref, rem_hbm,
+                  rem, x, t, r, u, sems):
     lane = lax.broadcasted_iota(jnp.int32, (64, 128), 1)
     sub = lax.broadcasted_iota(jnp.int32, (64, 128), 0)
     low = lane < 64
@@ -141,25 +148,30 @@
         for j in range(2):
             x[64 * i : 64 * i + 64, 384 + 128 * j : 512 + 128 * j] = eyes[i % 2] if i // 2 == j else jnp.zeros((64, 128), jnp.float32)
     r[...] = jnp.zeros_like(r)
-    def rest(i, v, wt):
-        lo, hi = 64 * i, 64 * i + 64
+    def keep(i, v):
+        lo = 64 * i
         tile, off = lo // 128 * 128, lo % 128
-        start, end = hi // 128 * 128, 384 + (hi + 127) // 128 * 128
-        ti = hdot(wt, x[lo:hi, start:end], ((1,), (0,)))
-        t[lo:hi, start:end] = ti
         own = jnp.where((lane - off >= sub) & ((lane >= 64) == (off > 0)), v, 0.0)
         if off == 0:
-            own = jnp.where(low, own, t[lo:hi, tile : tile + 128])
-        r[lo:hi, tile : tile + 128] = own
+            own = jnp.where(low, own, t[lo : lo + 64, tile : tile + 128])
+        r[lo : lo + 64, tile : tile + 128] = own
         if tile == 0:
-            r[lo:hi, 128:256] = t[lo:hi, 128:256]
-        if hi < 256:
-            down = hdot(ti[:, 0 : 256 - start], ti, ((0,), (0,)))
-            x[hi:256, start:end] -= down[hi - start :, :]
-        coup = t[lo:hi, 256:384]
-        coup_ref[lo:hi, :] = coup
-        wide = end - 384
-        part = hdot(t[lo:hi, 384:end], coup, ((0,), (0,)))
+            r[lo : lo + 64, 128:256] = t[lo : lo + 64, 128:256]
+        coup_ref[lo : lo + 64, :] = t[lo : lo + 64, 256:384]
+
+    def solve(i, wt):
+        lo, hi = 64 * i, 64 * i + 64
+        start, end = hi // 128 * 128, 384 + (hi + 127) // 128 * 128
+        t[lo:hi, start:end] = hdot(wt, x[lo:hi, start:end], ((1,), (0,)))
+
+    def reduce(lo, hi, first, last, start, end):
+        tile = first // 128 * 128
+        down = hdot(t[lo:hi, tile : tile + 128], t[lo:hi, start:end], ((0,), (0,)))
+        x[first:last, start:end] -= down[first - tile : last - tile, :]
+
+    def backward(lo, hi):
+        wide = (hi + 127) // 128 * 128
+        part = hdot(t[lo:hi, 384 : 384 + wide], t[lo:hi, 256:384], ((0,), (0,)))
         if wide < 256:
             part = jnp.concatenate([part, jnp.zeros((256 - wide, 128), jnp.float32)], axis=0)
         return part
@@ -167,28 +179,32 @@
     def next_block(i, wt):
         lo, hi = 64 * i, 64 * i + 64
         tile, off = hi // 128 * 128, hi % 128
-        ti = hdot(wt, x[lo:hi, tile : tile + 128], ((1,), (0,)))
+        t[lo:hi, tile : tile + 128] = hdot(wt, x[lo:hi, tile : tile + 128], ((1,), (0,)))
+        ti = t[0:hi, 128:256] if i == 1 else t[lo:hi, tile : tile + 128]
         down = hdot(ti, ti, ((0,), (0,)))
         return x[hi : hi + 64, tile : tile + 128] - down[off : off + 64, :]
 
-    update = None
     d = x[0:64, 0:128]
-    held = None
     for i in range(4):
         m = jnp.where(low, d, eyes[1]) if i % 2 == 0 else jnp.where(low, eyes[0], d)
         eliminate(m, 64 * (i % 2), u.at[i])
         v = u[i]
         wt = v[:, 64:128] if i % 2 == 0 else v[:, 0:64]
-        if held is not None:
-            part = rest(*held)
-            update = part if update is None else update + part
         if i < 3:
             d = next_block(i, wt)
-        held = (i, v, wt)
-    update = update + rest(*held)
+        solve(i, wt)
+        if i == 0:
+            reduce(0, 64, 64, 128, 128, 512)
+        elif i == 1:
+            reduce(0, 128, 128, 256, 128, 512)
+            update = backward(0, 128)
+        elif i == 2:
+            reduce(128, 192, 192, 256, 256, 640)
+            update = update + backward(128, 192)
+        else:
+            update = update + backward(192, 256)
+        keep(i, v)
     update = update.astype(jnp.bfloat16)
-    for load in loads:
-        load.wait()
     step = panel.shape[0] // CHUNKS
     stores = []
     for i in range(CHUNKS):
@@ -196,7 +212,7 @@
         rem[at, :] = (
             slab[at, :].astype(jnp.float32) - jnp.dot(panel[at, :], update, preferred_element_type=jnp.float32)
         ).astype(jnp.bfloat16)
-        store = pltpu.make_async_copy(rem.at[at, :], rem_hbm.at[at, :], sems.at[2 + i])
+        store = pltpu.make_async_copy(rem.at[at, :], rem_hbm.at[at, :], sems.at[i])
         store.start()
         stores.append(store)
     share = l_ref.shape[0]
@@ -214,7 +230,7 @@
     hbm = pl.BlockSpec(memory_space=pl.ANY)
     return pl.pallas_call(
         finish_kernel,
-        in_specs=[vmem, hbm, hbm],
+        in_specs=[vmem, vmem, vmem],
         out_specs=(vmem, vmem, hbm),
         out_shape=(
             jax.ShapeDtypeStruct((share, 256), jnp.float32),
@@ -222,16 +238,14 @@
             jax.ShapeDtypeStruct((rows, 128), jnp.bfloat16),
         ),
         scratch_shapes=[
-            pltpu.VMEM((rows, 256), jnp.bfloat16),
-            pltpu.VMEM((rows, 128), jnp.bfloat16),
             pltpu.VMEM((rows, 128), jnp.bfloat16),
             pltpu.VMEM((256, 640), jnp.float32),
             pltpu.VMEM((256, 640), jnp.float32),
             pltpu.VMEM((256, 256), jnp.float32),
             pltpu.VMEM((4, 64, 128), jnp.float32),
-            pltpu.SemaphoreType.DMA((2 + CHUNKS,)),
+            pltpu.SemaphoreType.DMA((CHUNKS,)),
         ],
-        compiler_params=pltpu.CompilerParams(vmem_limit_bytes=32 * 1024 * 1024),
+        compiler_params=pltpu.CompilerParams(vmem_limit_bytes=24 * 1024 * 1024),
         name="finish",
     )(sums, panel, slab)
 

time: 57.8 us -> 56.3 us (0.974)
  Pallas kernels: 13.7 us -> 12.2 us
    pallas_call x1, Pallas kernels: 10.1 us -> 8.58 us  [finish(): pl.pallas_call(finish_kernel, in_specs=[vmem, vmem, vmem], out_specs=(vme...]
where the time goes in v4:
time: 56.3 us; the launch traced here: 56 us
  blocking collectives  42.8 us (76%)
  Pallas kernels  12.2 us (22%)
  between operations  0.68 us (1%)
    all_to_all x2, blocking collectives, exchange(): return lax.all_to_all(parts, 'row', 0, 0, tiled=True)  42.8 us
    pallas_call x1, Pallas kernels, finish(): pl.pallas_call(finish_kernel, in_specs=[vmem, vmem, vmem], out_specs=(vme...  8.58 us
    pallas_call x1, Pallas kernels, local_sums(): pl.pallas_call(functools.partial(gather_kernel, scale, groups), in_specs=...  3.59 us

profile of v4, /device:TPU:1, one launch (start us, length us, event | category | flops | bytes accessed | tf_op | source)
XLA Modules:
  0.0 56.0 jit_solution(15716675925607918112)
XLA Ops:
  0.6 0.0 copy-start.1
  0.6 0.0 copy-start
  0.6 3.6 %sums.1 = f32[64,1,1152]{2,1,0:T(1,128)} custom-call(bf16[4096,256]{1,0:T(8,128)(2,1)} %panel.1, bf16[4096,128]{1,0:T(8,128)(2,1)} %slab.1), custom_call_target="tpu_custom_call" | custom-call | tf_op jit(solution)/shard_map/sums/pallas_call | solution.py:116
  4.2 24.3 %all_to_all.10 = f32[64,1,1152]{2,1,0:T(1,128)S(1)} all-to-all(f32[64,1,1152]{2,1,0:T(1,128)} %sums.1), channel_id=1, replica_groups=mesh['row'=64,'col'=8] {'row'}, dimensions={0} | all-to-all | bytes 589824 | tf_op jit(solution)/shard_map/all_to_all | solution.py:254
  28.5 0.2 reduce_sum.9
  28.7 0.2 broadcast_in_dim.2
  28.9 18.5 %all_to_all.11 = f32[64,1,1152]{2,1,0:T(1,128)S(1)} all-to-all(f32[64,1,1152]{2,1,0:T(1,128)S(1)} %broadcast_in_dim.2), channel_id=1, replica_groups=mesh['row'=64,'col'=8] {'row'}, dimensions={0} | all-to-all | bytes 589824 | tf_op jit(solution)/shard_map/all_to_all | solution.py:254
  47.4 0.0 copy-done.1
  47.5 0.0 copy-done
  47.5 8.6 %finish.1 = (f32[32,256]{1,0:T(8,128)}, f32[256,128]{1,0:T(8,128)}, bf16[4096,128]{1,0:T(8,128)(2,1)}) custom-call(f32[64,1152]{1,0:T(8,128)S(1)} %bitcast.4, bf16[4096,256]{1,0:T(8,128)(2,1)S(1)} %copy-done, bf16[4096,128]{1,0:T(8,128)(2,1)S(1)} %copy-done.1), custom_call_target="tpu_custom_call" | custom-call | tf_op jit(solution)/shard_map/finish/pallas_call | solution.py:231
  (1 shorter events, 0.0 us)
Async XLA Ops:
  0.6 46.8 %copy-start.1 = (bf16[4096,128]{1,0:T(8,128)(2,1)S(1)}, bf16[4096,128]{1,0:T(8,128)(2,1)}, u32[]{:S(2)}) copy-start(bf16[4096,128]{1,0:T(8,128)(2,1)} %slab.1) | copy-start | bytes 3145732
  0.6 46.8 %copy-start = (bf16[4096,256]{1,0:T(8,128)(2,1)S(1)}, bf16[4096,256]{1,0:T(8,128)(2,1)}, u32[]{:S(2)}) copy-start(bf16[4096,256]{1,0:T(8,128)(2,1)} %panel.1) | copy-start | bytes 6291460

commit v5 on v4

--- a/solution.py
+++ b/solution.py
@@ -115,9 +115,9 @@
     rows = panel.shape[0]
     return pl.pallas_call(
         functools.partial(gather_kernel, scale, groups),
-        in_specs=[pl.BlockSpec(memory_space=pl.ANY)] * 2,
+        in_specs=[pl.BlockSpec(memory_space=pltpu.HBM)] * 2,
         out_specs=pl.BlockSpec(memory_space=pltpu.VMEM),
-        out_shape=jax.ShapeDtypeStruct((64, 1, 1152), jnp.float32),
+        out_shape=pltpu.VMEM((64, 1, 1152), jnp.float32),
         scratch_shapes=[
             pltpu.VMEM((rows, 256), jnp.bfloat16),
             pltpu.VMEM((rows, 128), jnp.bfloat16),
@@ -132,8 +132,8 @@
 CHUNKS = 4
 
 
-def finish_kernel(s_ref, panel, slab, l_ref, coup_ref, rem_hbm,
-                  rem, x, t, r, u, sems):
+def finish_kernel(s_ref, panel, slab, l_hbm, coup_hbm, rem_hbm,
+                  l_ref, coup_ref, rem, x, t, r, u, sems):
     lane = lax.broadcasted_iota(jnp.int32, (64, 128), 1)
     sub = lax.broadcasted_iota(jnp.int32, (64, 128), 0)
     low = lane < 64
@@ -206,7 +206,17 @@
         keep(i, v)
     update = update.astype(jnp.bfloat16)
     step = panel.shape[0] // CHUNKS
-    stores = []
+    share = l_ref.shape[0]
+    pick = lax.broadcasted_iota(jnp.int32, (share, 256), 1) == (
+        lax.broadcasted_iota(jnp.int32, (share, 256), 0) + lax.axis_index("col") * share
+    )
+    l_ref[...] = hdot(pick.astype(jnp.float32), r[...], ((1,), (1,)))
+    stores = [
+        pltpu.make_async_copy(l_ref, l_hbm, sems.at[CHUNKS]),
+        pltpu.make_async_copy(coup_ref, coup_hbm, sems.at[CHUNKS + 1]),
+    ]
+    for store in stores:
+        store.start()
     for i in range(CHUNKS):
         at = pl.ds(i * step, step)
         rem[at, :] = (
@@ -215,11 +225,6 @@
         store = pltpu.make_async_copy(rem.at[at, :], rem_hbm.at[at, :], sems.at[i])
         store.start()
         stores.append(store)
-    share = l_ref.shape[0]
-    pick = lax.broadcasted_iota(jnp.int32, (share, 256), 1) == (
-        lax.broadcasted_iota(jnp.int32, (share, 256), 0) + lax.axis_index("col") * share
-    )
-    l_ref[...] = hdot(pick.astype(jnp.float32), r[...], ((1,), (1,)))
     for store in stores:
         store.wait()
 
@@ -231,19 +236,21 @@
     return pl.pallas_call(
         finish_kernel,
         in_specs=[vmem, vmem, vmem],
-        out_specs=(vmem, vmem, hbm),
+        out_specs=(hbm, hbm, hbm),
         out_shape=(
             jax.ShapeDtypeStruct((share, 256), jnp.float32),
             jax.ShapeDtypeStruct((256, 128), jnp.float32),
             jax.ShapeDtypeStruct((rows, 128), jnp.bfloat16),
         ),
         scratch_shapes=[
+            pltpu.VMEM((share, 256), jnp.float32),
+            pltpu.VMEM((256, 128), jnp.float32),
             pltpu.VMEM((rows, 128), jnp.bfloat16),
             pltpu.VMEM((256, 640), jnp.float32),
             pltpu.VMEM((256, 640), jnp.float32),
             pltpu.VMEM((256, 256), jnp.float32),
             pltpu.VMEM((4, 64, 128), jnp.float32),
-            pltpu.SemaphoreType.DMA((CHUNKS,)),
+            pltpu.SemaphoreType.DMA((CHUNKS + 2,)),
         ],
         compiler_params=pltpu.CompilerParams(vmem_limit_bytes=24 * 1024 * 1024),
         name="finish",

time: 56.3 us -> 54.6 us (0.970)
  Pallas kernels: 12.2 us -> 10.8 us
    pallas_call x1, Pallas kernels: 3.59 us -> 2.88 us  [local_sums(): pl.pallas_call(functools.partial(gather_kernel, scale, groups), in_specs=...]
    pallas_call x1, Pallas kernels: 8.58 us -> 7.92 us  [finish(): pl.pallas_call(finish_kernel, in_specs=[vmem, vmem, vmem], out_specs=(hbm...]
where the time goes in v5:
time: 54.6 us; the launch traced here: 54.5 us
  blocking collectives  42.6 us (78%)
  Pallas kernels  10.8 us (20%)
  between operations  0.68 us (1%)
    all_to_all x2, blocking collectives, exchange(): return lax.all_to_all(parts, 'row', 0, 0, tiled=True)  42.6 us
    pallas_call x1, Pallas kernels, finish(): pl.pallas_call(finish_kernel, in_specs=[vmem, vmem, vmem], out_specs=(hbm...  7.92 us
    pallas_call x1, Pallas kernels, local_sums(): pl.pallas_call(functools.partial(gather_kernel, scale, groups), in_specs=...  2.88 us

profile of v5, /device:TPU:1, one launch (start us, length us, event | category | flops | bytes accessed | tf_op | source)
XLA Modules:
  0.0 54.5 jit_solution(17000309569067439135)
XLA Ops:
  0.6 0.0 copy-start.1
  0.6 0.0 copy-start
  0.6 2.9 %sums.1 = f32[64,1,1152]{2,1,0:T(1,128)S(1)} custom-call(bf16[4096,256]{1,0:T(8,128)(2,1)} %panel.1, bf16[4096,128]{1,0:T(8,128)(2,1)} %slab.1), custom_call_target="tpu_custom_call" | custom-call | tf_op jit(solution)/shard_map/sums/pallas_call | solution.py:116
  3.5 24.1 %all_to_all.10 = f32[64,1,1152]{2,1,0:T(1,128)S(1)} all-to-all(f32[64,1,1152]{2,1,0:T(1,128)S(1)} %sums.1), channel_id=1, replica_groups=mesh['row'=64,'col'=8] {'row'}, dimensions={0} | all-to-all | bytes 589824 | tf_op jit(solution)/shard_map/all_to_all | solution.py:261
  27.6 0.2 reduce_sum.9
  27.8 0.2 broadcast_in_dim.2
  28.0 18.5 %all_to_all.11 = f32[64,1,1152]{2,1,0:T(1,128)S(1)} all-to-all(f32[64,1,1152]{2,1,0:T(1,128)S(1)} %broadcast_in_dim.2), channel_id=1, replica_groups=mesh['row'=64,'col'=8] {'row'}, dimensions={0} | all-to-all | bytes 589824 | tf_op jit(solution)/shard_map/all_to_all | solution.py:261
  46.5 0.0 copy-done.1
  46.5 0.0 copy-done
  46.5 7.9 %finish.1 = (f32[32,256]{1,0:T(8,128)}, f32[256,128]{1,0:T(8,128)}, bf16[4096,128]{1,0:T(8,128)(2,1)}) custom-call(f32[64,1152]{1,0:T(8,128)S(1)} %bitcast.4, bf16[4096,256]{1,0:T(8,128)(2,1)S(1)} %copy-done, bf16[4096,128]{1,0:T(8,128)(2,1)S(1)} %copy-done.1), custom_call_target="tpu_custom_call" | custom-call | tf_op jit(solution)/shard_map/finish/pallas_call | solution.py:236
  (1 shorter events, 0.0 us)
Async XLA Ops:
  0.6 45.9 %copy-start.1 = (bf16[4096,128]{1,0:T(8,128)(2,1)S(1)}, bf16[4096,128]{1,0:T(8,128)(2,1)}, u32[]{:S(2)}) copy-start(bf16[4096,128]{1,0:T(8,128)(2,1)} %slab.1) | copy-start | bytes 3145732
  0.6 45.9 %copy-start = (bf16[4096,256]{1,0:T(8,128)(2,1)S(1)}, bf16[4096,256]{1,0:T(8,128)(2,1)}, u32[]{:S(2)}) copy-start(bf16[4096,256]{1,0:T(8,128)(2,1)} %panel.1) | copy-start | bytes 6291460

commit v6 on v5

--- a/solution.py
+++ b/solution.py
@@ -129,7 +129,7 @@
     )(panel, slab)
 
 
-CHUNKS = 4
+CHUNKS = 8
 
 
 def finish_kernel(s_ref, panel, slab, l_hbm, coup_hbm, rem_hbm,
@@ -210,13 +210,7 @@
     pick = lax.broadcasted_iota(jnp.int32, (share, 256), 1) == (
         lax.broadcasted_iota(jnp.int32, (share, 256), 0) + lax.axis_index("col") * share
     )
-    l_ref[...] = hdot(pick.astype(jnp.float32), r[...], ((1,), (1,)))
-    stores = [
-        pltpu.make_async_copy(l_ref, l_hbm, sems.at[CHUNKS]),
-        pltpu.make_async_copy(coup_ref, coup_hbm, sems.at[CHUNKS + 1]),
-    ]
-    for store in stores:
-        store.start()
+    stores = []
     for i in range(CHUNKS):
         at = pl.ds(i * step, step)
         rem[at, :] = (
@@ -225,6 +219,12 @@
         store = pltpu.make_async_copy(rem.at[at, :], rem_hbm.at[at, :], sems.at[i])
         store.start()
         stores.append(store)
+        if i == 1:
+            l_ref[...] = hdot(pick.astype(jnp.float32), r[...], ((1,), (1,)))
+            for n, (source, target) in enumerate(((l_ref, l_hbm), (coup_ref, coup_hbm))):
+                store = pltpu.make_async_copy(source, target, sems.at[CHUNKS + n])
+                store.start()
+                stores.append(store)
     for store in stores:
         store.wait()
 

time: 54.6 us -> 54.8 us (level)
  no operation moved by 1% of the time
where the time goes in v6:
time: 54.8 us; the launch traced here: 54.6 us
  blocking collectives  42.6 us (78%)
  Pallas kernels  10.9 us (20%)
  between operations  0.68 us (1%)
    all_to_all x2, blocking collectives, exchange(): return lax.all_to_all(parts, 'row', 0, 0, tiled=True)  42.6 us
    pallas_call x1, Pallas kernels, finish(): pl.pallas_call(finish_kernel, in_specs=[vmem, vmem, vmem], out_specs=(hbm...  8.05 us
    pallas_call x1, Pallas kernels, local_sums(): pl.pallas_call(functools.partial(gather_kernel, scale, groups), in_specs=...  2.88 us

profile of v6, /device:TPU:1, one launch (start us, length us, event | category | flops | bytes accessed | tf_op | source)
XLA Modules:
  0.0 54.6 jit_solution(8814410935890180893)
XLA Ops:
  0.6 0.0 copy-start.1
  0.6 0.0 copy-start
  0.6 2.9 %sums.1 = f32[64,1,1152]{2,1,0:T(1,128)S(1)} custom-call(bf16[4096,256]{1,0:T(8,128)(2,1)} %panel.1, bf16[4096,128]{1,0:T(8,128)(2,1)} %slab.1), custom_call_target="tpu_custom_call" | custom-call | tf_op jit(solution)/shard_map/sums/pallas_call | solution.py:116
  3.5 24.1 %all_to_all.10 = f32[64,1,1152]{2,1,0:T(1,128)S(1)} all-to-all(f32[64,1,1152]{2,1,0:T(1,128)S(1)} %sums.1), channel_id=1, replica_groups=mesh['row'=64,'col'=8] {'row'}, dimensions={0} | all-to-all | bytes 589824 | tf_op jit(solution)/shard_map/all_to_all | solution.py:261
  27.6 0.2 reduce_sum.9
  27.8 0.2 broadcast_in_dim.2
  28.0 18.5 %all_to_all.11 = f32[64,1,1152]{2,1,0:T(1,128)S(1)} all-to-all(f32[64,1,1152]{2,1,0:T(1,128)S(1)} %broadcast_in_dim.2), channel_id=1, replica_groups=mesh['row'=64,'col'=8] {'row'}, dimensions={0} | all-to-all | bytes 589824 | tf_op jit(solution)/shard_map/all_to_all | solution.py:261
  46.5 0.0 copy-done.1
  46.5 0.0 copy-done
  46.5 8.1 %finish.1 = (f32[32,256]{1,0:T(8,128)}, f32[256,128]{1,0:T(8,128)}, bf16[4096,128]{1,0:T(8,128)(2,1)}) custom-call(f32[64,1152]{1,0:T(8,128)S(1)} %bitcast.4, bf16[4096,256]{1,0:T(8,128)(2,1)S(1)} %copy-done, bf16[4096,128]{1,0:T(8,128)(2,1)S(1)} %copy-done.1), custom_call_target="tpu_custom_call" | custom-call | tf_op jit(solution)/shard_map/finish/pallas_call | solution.py:236
  (1 shorter events, 0.0 us)
Async XLA Ops:
  0.6 45.9 %copy-start.1 = (bf16[4096,128]{1,0:T(8,128)(2,1)S(1)}, bf16[4096,128]{1,0:T(8,128)(2,1)}, u32[]{:S(2)}) copy-start(bf16[4096,128]{1,0:T(8,128)(2,1)} %slab.1) | copy-start | bytes 3145732
  0.6 45.9 %copy-start = (bf16[4096,256]{1,0:T(8,128)(2,1)S(1)}, bf16[4096,256]{1,0:T(8,128)(2,1)}, u32[]{:S(2)}) copy-start(bf16[4096,256]{1,0:T(8,128)(2,1)} %panel.1) | copy-start | bytes 6291460
